TPU v7x, 32 devices: a whole 2x2x4 slice. The times are simulated.
32 devices in a mesh: dp: 4 (over y, x), rows: 8 (over z, core).
Axes of the slice: x: 2, y: 2, z: 4, core: 2. Of those that a mesh axis runs over, the one named last changes fastest.
Arguments:
- images: float32 [8192, 1152], P(('dp', 'rows')), may hold values from -0.2 to 0.2
- texts: float32 [8192, 1152], P(('dp', 'rows')), may hold values from -0.2 to 0.2
- log_temp: float32 [1], replicated, may hold values from 0.7 to 1.8
- bias: float32 [1], replicated, may hold values from -3 to -1
Outputs:
- row_loss: float32 [8192], P(('dp', 'rows'))
- image_grad: float32 [8192, 1152], P(('dp', 'rows'))
- text_grad: float32 [8192, 1152], P(('dp', 'rows'))
All inputs are finite; a program needn't handle non-finite values.
Results may differ from a plain program's by a relative error of at most 0.0091.
Values may be sent and summed in bfloat16 or wider, within the bound.
A program may use at most 64 MiB of HBM per device.

v0:
```python
import jax
import jax.numpy as jnp
from jax import lax
from jax.sharding import PartitionSpec as P

STEPS = 4


def from_behind(value, axis, steps):
    count = lax.axis_size(axis)
    pairs = [(source, (source + steps) % count) for source in range(count)]
    return lax.ppermute(value, axis, pairs)


def unit_rows(values):
    norms = jnp.sqrt(jnp.sum(values * values, axis=-1, keepdims=True) + 1e-06)
    return (values / norms, norms)


def back_rows(unit, norms, grad_unit):
    along = jnp.sum(unit * grad_unit, axis=-1, keepdims=True)
    return (grad_unit - unit * along) / norms


def local(images, texts, log_temp, bias):
    scale = jnp.exp(log_temp[0])
    shift_b = bias[0]
    img_unit, img_norm = unit_rows(images)
    txt_unit, txt_norm = unit_rows(texts)
    img_half = img_unit.astype(jnp.bfloat16)
    txt_half = txt_unit.astype(jnp.bfloat16)
    count = images.shape[0]
    eye = jnp.eye(count, dtype=jnp.float32)

    def tile_grad(left, visit, first):
        logits = scale * jnp.dot(left, visit.T, preferred_element_type=jnp.float32) + shift_b
        sign = 2.0 * eye - 1.0 if first else -jnp.ones_like(eye)
        loss_part = jnp.sum(jax.nn.softplus(-sign * logits), axis=-1)
        dlogit = (-sign * jax.nn.sigmoid(-sign * logits) * scale).astype(jnp.bfloat16)
        return (loss_part, dlogit)

    def score_tile(visit, first):
        loss_part, dlogit = tile_grad(img_half, visit, first)
        img_part = jnp.dot(dlogit, visit, preferred_element_type=jnp.float32)
        txt_part = jnp.dot(dlogit.T, img_half, preferred_element_type=jnp.float32)
        return (loss_part, img_part, txt_part)

    loss_sum, img_grad_unit, own_txt = score_tile(txt_half, True)
    current = txt_half
    carried = own_txt
    for step in range(1, STEPS):
        current = from_behind(current, ("dp", "rows"), 1)
        carried = from_behind(carried, ("dp", "rows"), 1)
        loss_part, img_part, txt_part = score_tile(current, False)
        loss_sum = loss_sum + loss_part
        img_grad_unit = img_grad_unit + img_part
        carried = carried + txt_part
    txt_grad_unit = from_behind(carried, ("dp", "rows"), 1 - STEPS)
    row_loss = loss_sum / (STEPS * count)
    image_grad = back_rows(img_unit, img_norm, img_grad_unit)
    text_grad = back_rows(txt_unit, txt_norm, txt_grad_unit)
    return (row_loss, image_grad, text_grad)


def solution(mesh):
    placed = (P(("dp", "rows"), None), P(("dp", "rows"), None), P(), P())
    return jax.shard_map(
        local,
        mesh=mesh,
        in_specs=placed,
        out_specs=(P(("dp", "rows")), P(("dp", "rows"), None), P(("dp", "rows"), None)),
        check_vma=False,
    )
```

profile of v0, /device:TPU:3, one launch (start us, length us, event | category | flops | bytes accessed | tf_op | source)
XLA Modules:
  0.0 123.2 jit_solution(1661323520928796837)
XLA Ops:
  0.6 0.0 copy-start.1
  1.4 1.4 %multiply_reduce_fusion.3 = f32[256]{0:T(256)S(1)} fusion(f32[256,1152]{1,0:T(8,128)} %param.4), kind=kLoop, calls=%fused_computation.9 | loop fusion | flops 589568 | bytes 1180672 | tf_op jit(solution)/shard_map/reduce_sum | solution.py:16
  2.8 0.0 copy-start
  2.8 0.0 copy-done.1
  2.8 0.1 fusion.13
  3.0 1.1 copy-done
  4.1 0.2 multiply_reduce_fusion.2
  4.3 0.2 fusion.14
  5.1 0.5 fusion.5
  5.6 0.4 fusion.11
  6.0 1.9 %collective-permute-start.3 = (f32[256,1152]{1,0:T(8,128)S(1)}, f32[256,1152]{1,0:T(8,128)S(1)}, u32[]{:S(2)}, u32[]{:S(2)}) collective-permute-start(f32[256,1152]{1,0:T(8,128)S(1)} %fusion.11), channel_id=1, source_target_pairs={{0,1},{1,2},{2,3},{3,4},{4,5},{5,6},{6,7},{7,8},{8,9},{9,10},{10,1... | collective-permute-start | bytes 3538952 | tf_op jit(solution)/shard_map/ppermute | solution.py:12
  7.9 0.1 collective-permute-start
  8.0 19.4 %collective-permute-done = bf16[256,1152]{1,0:T(8,128)(2,1)S(1)} collective-permute-done((bf16[256,1152]{1,0:T(8,128)(2,1)S(1)}, bf16[256,1152]{1,0:T(8,128)(2,1)S(1)}, u32[]{:S(2)}, u32[]{:S(2)}) %collective-permute-start) | collective-permute-done | bytes 589856 | tf_op jit(solution)/shard_map/ppermute | solution.py:12
  27.4 0.5 fusion.6
  27.9 0.0 collective-permute-done.3
  27.9 0.4 convolution_add_fusion
  28.3 2.5 %collective-permute-start.4 = (f32[256,1152]{1,0:T(8,128)S(1)}, f32[256,1152]{1,0:T(8,128)S(1)}, u32[]{:S(2)}, u32[]{:S(2)}) collective-permute-start(f32[256,1152]{1,0:T(8,128)S(1)} %convolution_add_fusion), channel_id=1, source_target_pairs={{0,1},{1,2},{2,3},{3,4},{4,5},{5,6},{6,7},{7,8},{8,9},{9,10},{10,1... | collective-permute-start | bytes 3538952 | tf_op jit(solution)/shard_map/ppermute | solution.py:12
  30.8 0.1 collective-permute-start.1
  30.9 19.4 %collective-permute-done.1 = bf16[256,1152]{1,0:T(8,128)(2,1)S(1)} collective-permute-done((bf16[256,1152]{1,0:T(8,128)(2,1)S(1)}, bf16[256,1152]{1,0:T(8,128)(2,1)S(1)}, u32[]{:S(2)}, u32[]{:S(2)}) %collective-permute-start.1) | collective-permute-done | bytes 589856 | tf_op jit(solution)/shard_map/ppermute | solution.py:12
  50.3 0.5 fusion.7
  50.8 0.4 fusion.9
  51.1 0.0 collective-permute-done.4
  51.1 0.1 add.109
  51.3 2.5 %collective-permute-start.5 = (f32[256,1152]{1,0:T(8,128)S(1)}, f32[256,1152]{1,0:T(8,128)S(1)}, u32[]{:S(2)}, u32[]{:S(2)}) collective-permute-start(f32[256,1152]{1,0:T(8,128)S(1)} %add.109), channel_id=1, source_target_pairs={{0,1},{1,2},{2,3},{3,4},{4,5},{5,6},{6,7},{7,8},{8,9},{9,10},{10,1... | collective-permute-start | bytes 3538952 | tf_op jit(solution)/shard_map/ppermute | solution.py:12
  53.8 0.4 fusion.12
  54.2 0.1 collective-permute-start.2
  54.3 0.4 convolution_add_fusion.3
  54.7 0.4 convolution_add_fusion.2
  55.1 18.2 %collective-permute-done.2 = bf16[256,1152]{1,0:T(8,128)(2,1)S(1)} collective-permute-done((bf16[256,1152]{1,0:T(8,128)(2,1)S(1)}, bf16[256,1152]{1,0:T(8,128)(2,1)S(1)}, u32[]{:S(2)}, u32[]{:S(2)}) %collective-permute-start.2) | collective-permute-done | bytes 589856 | tf_op jit(solution)/shard_map/ppermute | solution.py:12
  73.3 0.5 fusion.8
  73.8 0.4 fusion.10
  74.1 0.0 collective-permute-done.5
  74.1 0.1 add.110
  74.3 4.6 %collective-permute-start.6 = (f32[256,1152]{1,0:T(8,128)S(1)}, f32[256,1152]{1,0:T(8,128)S(1)}, u32[]{:S(2)}, u32[]{:S(2)}) collective-permute-start(f32[256,1152]{1,0:T(8,128)S(1)} %add.110), channel_id=1, source_target_pairs={{0,29},{1,30},{2,31},{3,0},{4,1},{5,2},{6,3},{7,4},{8,5},{9,6},{10... | collective-permute-start | bytes 3538952 | tf_op jit(solution)/shard_map/ppermute | solution.py:12
  78.8 0.6 add_multiply_fusion
  79.4 0.5 multiply_reduce_fusion.1
  79.9 1.3 %subtract_divide_fusion.1 = f32[256,1152]{1,0:T(8,128)} fusion(f32[256,1152]{1,0:T(8,128)S(1)} %get-tuple-element.12, f32[256]{0:T(256)S(1)} %get-tuple-element.11, f32[256]{0:T(256)S(1)} %add_sqrt_fusion.1, f32[256,1152]{1,0:T(8,128)S(1)} %copy-done.1), kind=kLoop, calls=%fused_computation.6 | loop fusion | flops 1179648 | bytes 3540992 | tf_op jit(solution)/shard_map/div | solution.py:22
  81.2 40.5 %collective-permute-done.6 = f32[256,1152]{1,0:T(8,128)S(1)} collective-permute-done((f32[256,1152]{1,0:T(8,128)S(1)}, f32[256,1152]{1,0:T(8,128)S(1)}, u32[]{:S(2)}, u32[]{:S(2)}) %collective-permute-start.6) | collective-permute-done | bytes 1179680 | tf_op jit(solution)/shard_map/ppermute | solution.py:12
  121.7 0.3 multiply_reduce_fusion
  122.0 1.3 %subtract_divide_fusion = f32[256,1152]{1,0:T(8,128)} fusion(f32[256,1152]{1,0:T(8,128)S(1)} %collective-permute-done.6, f32[256]{0:T(256)S(1)} %multiply_reduce_fusion, f32[256]{0:T(256)S(1)} %add_sqrt_fusion, f32[256,1152]{1,0:T(8,128)S(1)} %copy-done), kind=kLoop, calls=%fused_computation.4 | loop fusion | flops 1179648 | bytes 3540992 | tf_op jit(solution)/shard_map/div | solution.py:22
  (2 shorter events, 0.0 us)
Async XLA Ops:
  0.6 2.2 %copy-start.1 = (f32[256,1152]{1,0:T(8,128)S(1)}, f32[256,1152]{1,0:T(8,128)}, u32[]{:S(2)}) copy-start(f32[256,1152]{1,0:T(8,128)} %param.4) | copy-start | bytes 3538948
  2.8 1.3 %copy-start = (f32[256,1152]{1,0:T(8,128)S(1)}, f32[256,1152]{1,0:T(8,128)}, u32[]{:S(2)}) copy-start(f32[256,1152]{1,0:T(8,128)} %param.5) | copy-start | bytes 3538948
  6.0 21.9 %collective-permute-start.3 = (f32[256,1152]{1,0:T(8,128)S(1)}, f32[256,1152]{1,0:T(8,128)S(1)}, u32[]{:S(2)}, u32[]{:S(2)}) collective-permute-start(f32[256,1152]{1,0:T(8,128)S(1)} %fusion.11), channel_id=1, source_target_pairs={{0,1},{1,2},{2,3},{3,4},{4,5},{5,6},{6,7},{7,8},{8,9},{9,10},{10,1... | collective-permute-start | bytes 3538952 | tf_op jit(solution)/shard_map/ppermute | solution.py:12
  7.9 19.5 %collective-permute-start = (bf16[256,1152]{1,0:T(8,128)(2,1)S(1)}, bf16[256,1152]{1,0:T(8,128)(2,1)S(1)}, u32[]{:S(2)}, u32[]{:S(2)}) collective-permute-start(bf16[256,1152]{1,0:T(8,128)(2,1)S(1)} %fusion.14), channel_id=1, source_target_pairs={{0,1},{1,2},{2,3},{3,4},{4,5},{5,6},{6,7},{7,8},{8,9},{9,10},{10,1... | collective-permute-start | bytes 1769480 | tf_op jit(solution)/shard_map/ppermute | solution.py:12
  28.3 22.9 %collective-permute-start.4 = (f32[256,1152]{1,0:T(8,128)S(1)}, f32[256,1152]{1,0:T(8,128)S(1)}, u32[]{:S(2)}, u32[]{:S(2)}) collective-permute-start(f32[256,1152]{1,0:T(8,128)S(1)} %convolution_add_fusion), channel_id=1, source_target_pairs={{0,1},{1,2},{2,3},{3,4},{4,5},{5,6},{6,7},{7,8},{8,9},{9,10},{10,1... | collective-permute-start | bytes 3538952 | tf_op jit(solution)/shard_map/ppermute | solution.py:12
  30.8 19.5 %collective-permute-start.1 = (bf16[256,1152]{1,0:T(8,128)(2,1)S(1)}, bf16[256,1152]{1,0:T(8,128)(2,1)S(1)}, u32[]{:S(2)}, u32[]{:S(2)}) collective-permute-start(bf16[256,1152]{1,0:T(8,128)(2,1)S(1)} %collective-permute-done), channel_id=1, source_target_pairs={{0,1},{1,2},{2,3},{3,4},{4,5},{5,6},{6,7},{7,8},{8,9},{9,10},{10,1... | collective-permute-start | bytes 1769480 | tf_op jit(solution)/shard_map/ppermute | solution.py:12
  51.3 22.9 %collective-permute-start.5 = (f32[256,1152]{1,0:T(8,128)S(1)}, f32[256,1152]{1,0:T(8,128)S(1)}, u32[]{:S(2)}, u32[]{:S(2)}) collective-permute-start(f32[256,1152]{1,0:T(8,128)S(1)} %add.109), channel_id=1, source_target_pairs={{0,1},{1,2},{2,3},{3,4},{4,5},{5,6},{6,7},{7,8},{8,9},{9,10},{10,1... | collective-permute-start | bytes 3538952 | tf_op jit(solution)/shard_map/ppermute | solution.py:12
  54.2 19.1 %collective-permute-start.2 = (bf16[256,1152]{1,0:T(8,128)(2,1)S(1)}, bf16[256,1152]{1,0:T(8,128)(2,1)S(1)}, u32[]{:S(2)}, u32[]{:S(2)}) collective-permute-start(bf16[256,1152]{1,0:T(8,128)(2,1)S(1)} %collective-permute-done.1), channel_id=1, source_target_pairs={{0,1},{1,2},{2,3},{3,4},{4,5},{5,6},{6,7},{7,8},{8,9},{9,10},{10,1... | collective-permute-start | bytes 1769480 | tf_op jit(solution)/shard_map/ppermute | solution.py:12
  74.3 47.4 %collective-permute-start.6 = (f32[256,1152]{1,0:T(8,128)S(1)}, f32[256,1152]{1,0:T(8,128)S(1)}, u32[]{:S(2)}, u32[]{:S(2)}) collective-permute-start(f32[256,1152]{1,0:T(8,128)S(1)} %add.110), channel_id=1, source_target_pairs={{0,29},{1,30},{2,31},{3,0},{4,1},{5,2},{6,3},{7,4},{8,5},{9,6},{10... | collective-permute-start | bytes 3538952 | tf_op jit(solution)/shard_map/ppermute | solution.py:12
where the time goes:
time: 123 us
  waiting for transfers between devices  97.5 us (79%)
  starting transfers between devices  11.7 us (10%)
  other arithmetic  5.5 us (4%)
  matrix products  5.23 us (4%)
  between operations  2.19 us (2%)
    ppermute x7, waiting for transfers between devices, from_behind(): return lax.ppermute(value, axis, pairs)  97.5 us
    ppermute x7, starting transfers between devices, from_behind(): return lax.ppermute(value, axis, pairs)  11.7 us
    div x2, other arithmetic, back_rows(): return (grad_unit - unit * along) / norms  2.52 us
  transfers between devices with their start and end apart: 7, of which 4 were waited for; matrix products, arithmetic and copies ran while one was open for 5% of the time, Pallas kernels for 0%

commit v1 on v0

v1 whole, which is shorter than its diff:
```python
import functools

import jax
import jax.numpy as jnp
from jax import lax
from jax.experimental import pallas as pl
from jax.experimental.pallas import tpu as pltpu
from jax.sharding import PartitionSpec as P

STEPS = 4
CHUNKS = 8
MESH = pl.DeviceIdType.MESH


def kernel(img_hbm, txt_hbm, temp_ref, bias_ref, loss_ref, gimg_ref, gtxt_ref,
           xin, own, buf, acc, losses, inv, in_sem, send_sem, recv_sem, out_sem):
    rows_n = lax.axis_size("rows")
    total = lax.axis_size("dp") * rows_n
    me = lax.axis_index("dp") * rows_n + lax.axis_index("rows")
    p = lax.rem(me, 2)
    q = 1 - p
    d = 1 - 2 * p
    count = own.shape[1]
    part = count // CHUNKS

    def peer(offset):
        place = lax.rem(me + offset * d + total, total)
        return (lax.div(place, rows_n), lax.rem(place, rows_n))

    barrier = pltpu.get_barrier_semaphore()
    for offset in (1, 2, 3, -1, -2):
        pl.semaphore_signal(barrier, inc=1, device_id=peer(offset), device_id_type=MESH)

    loads = [pltpu.make_async_copy(txt_hbm, xin.at[0], in_sem.at[0]),
             pltpu.make_async_copy(img_hbm, xin.at[1], in_sem.at[1])]
    for load in loads:
        load.start()

    def normalise(kind):
        values = xin[kind]
        scale_back = 1.0 / jnp.sqrt(jnp.sum(values * values, axis=-1, keepdims=True) + 1e-06)
        inv[kind] = jnp.broadcast_to(scale_back, inv.shape[1:])
        own[kind] = (values * scale_back).astype(jnp.bfloat16)

    def rows_of(i):
        return pl.ds(i * part, part)

    def remote(src, kind, slot, rows, number, i, offset):
        return pltpu.make_async_remote_copy(
            src_ref=src.at[rows], dst_ref=buf.at[kind, slot, rows],
            send_sem=send_sem.at[number, i], recv_sem=recv_sem.at[kind, slot, i],
            device_id=peer(offset), device_id_type=MESH)

    def landed(kind, slot, rows, i):
        pltpu.make_async_remote_copy(
            src_ref=buf.at[kind, slot, rows], dst_ref=buf.at[kind, slot, rows],
            send_sem=send_sem.at[0, i], recv_sem=recv_sem.at[kind, slot, i],
            device_id=peer(1), device_id_type=MESH).wait_recv()

    everything = pl.ds(0, count)
    scale = jnp.exp(temp_ref[...])
    shift = bias_ref[...]

    def tile(kind, visit, first):
        other = visit[...]
        dots = lax.dot_general(own[1 - kind], other, (((1,), (1,)), ((), ())),
                               preferred_element_type=jnp.float32)
        z = scale * dots + shift
        if first:
            eye = (lax.broadcasted_iota(jnp.int32, z.shape, 0)
                   == lax.broadcasted_iota(jnp.int32, z.shape, 1))
            z = jnp.where(eye, -z, z)
        e = jnp.exp(z)
        more = 1.0 + e
        soft = jnp.log(more)
        slope = (e / more) * scale
        if first:
            slope = jnp.where(eye, -slope, slope)
        half = soft.shape[1] // 2
        folded = soft[:, :half] + soft[:, half:]
        grad = jnp.dot(slope.astype(jnp.bfloat16), other, preferred_element_type=jnp.float32)
        if first:
            losses[kind] = folded
            acc[kind] = grad
        else:
            losses[kind] = losses[kind] + folded
            acc[kind] = acc[kind] + grad

    sent = []

    def send(copy):
        copy.start()
        sent.append(copy)

    pltpu.make_async_copy(txt_hbm, xin.at[q], in_sem.at[q]).wait()
    normalise(q)
    pl.semaphore_wait(barrier, 5)
    for i in range(CHUNKS):
        send(remote(own.at[q], q, 0, rows_of(i), 0, i, -1))
    pltpu.make_async_copy(txt_hbm, xin.at[p], in_sem.at[p]).wait()
    normalise(p)
    send(remote(own.at[p], p, 0, everything, 1, 0, 1))

    tile(0, own.at[0], True)
    tile(1, own.at[1], True)
    landed(q, 0, everything, 0)
    tile(q, buf.at[q, 0], False)

    for i in range(CHUNKS):
        rows = rows_of(i)
        landed(p, 0, rows, i)
        send(remote(buf.at[p, 0], p, 2, rows, 2, i, 2))
        send(remote(buf.at[p, 0], p, 1, rows, 3, i, 1))
        send(remote(own.at[p], p, 2, rows, 4, i, 3))
        if i > 0:
            landed(q, 2, rows_of(i - 1), i - 1)
            send(remote(buf.at[q, 2], q, 1, rows_of(i - 1), 5, i - 1, 1))
    tile(p, buf.at[p, 0], False)
    landed(q, 2, rows_of(CHUNKS - 1), CHUNKS - 1)
    send(remote(buf.at[q, 2], q, 1, rows_of(CHUNKS - 1), 5, CHUNKS - 1, 1))
    for kind, slot in ((q, 1), (q, 2), (p, 1), (p, 2)):
        if (kind is q and slot == 2) is False:
            for i in range(CHUNKS):
                landed(kind, slot, rows_of(i), i)
        tile(kind, buf.at[kind, slot], False)

    loss_ref[...] = jnp.sum(losses[0].T, axis=0, keepdims=True) / (STEPS * count)
    for kind, out in ((0, gimg_ref), (1, gtxt_ref)):
        factor = inv[1 - kind][:, :1]
        unit = xin[1 - kind] * factor
        grad = acc[kind]
        along = jnp.sum(unit * grad, axis=-1, keepdims=True)
        out[...] = (grad - unit * along) * factor
    for copy in sent:
        copy.wait_send()


def local(images, texts, log_temp, bias):
    count, width = images.shape
    block = jax.ShapeDtypeStruct((count, width), jnp.float32)
    vmem = pl.BlockSpec(memory_space=pltpu.VMEM)
    hbm = pl.BlockSpec(memory_space=pl.ANY)
    loss, gimg, gtxt = pl.pallas_call(
        kernel,
        out_shape=(jax.ShapeDtypeStruct((1, count), jnp.float32), block, block),
        in_specs=[hbm, hbm, vmem, vmem],
        out_specs=(vmem, vmem, vmem),
        scratch_shapes=[
            pltpu.VMEM((2, count, width), jnp.float32),
            pltpu.VMEM((2, count, width), jnp.bfloat16),
            pltpu.VMEM((2, STEPS - 1, count, width), jnp.bfloat16),
            pltpu.VMEM((2, count, width), jnp.float32),
            pltpu.VMEM((2, count, count // 2), jnp.float32),
            pltpu.VMEM((2, count, 128), jnp.float32),
            pltpu.SemaphoreType.DMA((2,)),
            pltpu.SemaphoreType.DMA((6, CHUNKS)),
            pltpu.SemaphoreType.DMA((2, STEPS - 1, CHUNKS)),
            pltpu.SemaphoreType.DMA((2,)),
        ],
        compiler_params=pltpu.CompilerParams(
            collective_id=0, has_side_effects=True, vmem_limit_bytes=48 * 1024 * 1024),
    )(images, texts, log_temp.reshape(1, 1), bias.reshape(1, 1))
    return (loss.reshape(count), gimg, gtxt)


def solution(mesh):
    placed = (P(("dp", "rows"), None), P(("dp", "rows"), None), P(), P())
    return jax.shard_map(
        local,
        mesh=mesh,
        in_specs=placed,
        out_specs=(P(("dp", "rows")), P(("dp", "rows"), None), P(("dp", "rows"), None)),
        check_vma=False,
    )
```

time: 123 us -> 60 us (0.49)
  the two profiles are of different devices: /device:TPU:3 before, /device:TPU:0 now
where the time goes in v1:
time: 60 us; the launch traced here: 59.7 us
  Pallas kernels  52.7 us (88%)
  local copies, waits for them, and re-layouts  5.12 us (9%)
  between operations  1.94 us (3%)
    pallas_call x1, Pallas kernels, local(): pl.pallas_call(kernel, out_shape=(jax.ShapeDtypeStruct((1, count), jnp.fl...  52.7 us
    unnamed x7, local copies, waits for them, and re-layouts  5.12 us

profile of v1, /device:TPU:0, one launch (start us, length us, event | category | flops | bytes accessed | tf_op | source)
XLA Modules:
  0.0 59.7 jit_solution(15905861101817764162)
XLA Ops:
  1.9 0.0 copy-start
  1.9 1.3 %copy-done = f32[256,1152]{1,0:T(8,128)S(1)} copy-done((f32[256,1152]{1,0:T(8,128)S(1)}, f32[256,1152]{1,0:T(8,128)}, u32[]{:S(2)}) %copy-start) | copy-done | bytes 1179672
  3.2 0.0 copy-start.1
  3.2 1.3 %copy-done.1 = f32[256,1152]{1,0:T(8,128)S(1)} copy-done((f32[256,1152]{1,0:T(8,128)S(1)}, f32[256,1152]{1,0:T(8,128)}, u32[]{:S(2)}) %copy-start.1) | copy-done | bytes 1179672
  4.5 52.7 %shard_map.67 = (f32[1,256]{1,0:T(1,128)S(1)}, f32[256,1152]{1,0:T(8,128)S(1)}, f32[256,1152]{1,0:T(8,128)S(1)}) custom-call(f32[256,1152]{1,0:T(8,128)S(1)} %copy-done, f32[256,1152]{1,0:T(8,128)S(1)} %copy-done.1, f32[1,1]{1,0:T(1,128)} %bitcast.3.temp_ref, f32[1,1]{1,0:T(1,128)} %bitcast.4.bias_ref), custom_call_target="tpu_custom_call" | custom-call | tf_op jit(solution)/shard_map/pallas_call | solution.py:143
  57.1 0.6 copy.12
  57.7 1.0 %copy.13 = f32[256,1152]{1,0:T(8,128)} copy(f32[256,1152]{1,0:T(8,128)S(1)} %get-tuple-element.13) | data formatting | bytes 2359296
  58.7 1.0 %copy.14 = f32[256,1152]{1,0:T(8,128)} copy(f32[256,1152]{1,0:T(8,128)S(1)} %get-tuple-element.14) | data formatting | bytes 2359296
Async XLA Ops:
  1.9 1.3 %copy-start = (f32[256,1152]{1,0:T(8,128)S(1)}, f32[256,1152]{1,0:T(8,128)}, u32[]{:S(2)}) copy-start(f32[256,1152]{1,0:T(8,128)} %img_hbm.1) | copy-start | bytes 3538948
  3.2 1.3 %copy-start.1 = (f32[256,1152]{1,0:T(8,128)S(1)}, f32[256,1152]{1,0:T(8,128)}, u32[]{:S(2)}) copy-start(f32[256,1152]{1,0:T(8,128)} %txt_hbm.1) | copy-start | bytes 3538948

commit v2 on v1

v2 whole, which is shorter than its diff:
```python
import functools

import jax
import jax.numpy as jnp
from jax import lax
from jax.experimental import pallas as pl
from jax.experimental.pallas import tpu as pltpu
from jax.sharding import PartitionSpec as P

STEPS = 4
CHUNKS = 8
HALVES = 2
LOADS = 4
PEERS = (1, 2, 3, -1, -2, -3)
MESH = pl.DeviceIdType.MESH


def kernel(img_hbm, txt_hbm, temp_ref, bias_ref, loss_ref, gimg_ref, gtxt_ref,
           xin, own, buf, acc, losses, inv, in_sem, send_sem, recv_sem):
    rows_n = lax.axis_size("rows")
    total = lax.axis_size("dp") * rows_n
    me = lax.axis_index("dp") * rows_n + lax.axis_index("rows")
    p = lax.rem(me, 2)
    q = 1 - p
    d = 1 - 2 * p
    count = own.shape[1]
    part = count // CHUNKS

    def peer(offset):
        place = lax.rem(me + offset * d + total, total)
        return (lax.div(place, rows_n), lax.rem(place, rows_n))

    barrier = pltpu.get_barrier_semaphore()
    for offset in PEERS:
        pl.semaphore_signal(barrier, inc=1, device_id=peer(offset), device_id_type=MESH)

    piece = count // LOADS

    def loading(source, kind, j):
        rows = pl.ds(j * piece, piece)
        return pltpu.make_async_copy(source.at[rows], xin.at[kind, rows], in_sem.at[kind, j])

    for j in range(LOADS):
        loading(txt_hbm, 0, j).start()
        loading(img_hbm, 1, j).start()

    def normalise(kind, j):
        rows = pl.ds(j * piece, piece)
        loading(txt_hbm, kind, j).wait()
        values = xin[kind, rows]
        scale_back = 1.0 / jnp.sqrt(jnp.sum(values * values, axis=-1, keepdims=True) + 1e-06)
        inv[kind, rows] = jnp.broadcast_to(scale_back, (piece, inv.shape[2]))
        own[kind, rows] = (values * scale_back).astype(jnp.bfloat16)

    line = rows_n // 2
    spot = lax.rem(lax.div(me, 2), line)

    def crosses(at, way):
        return jnp.logical_or(at + way < 0, at + way >= line)

    leaving = crosses(spot, d)
    early = jnp.logical_or(leaving, crosses(spot, -d))
    direct = crosses(lax.rem(spot - d + line, line), -d)

    def rows_of(i):
        return pl.ds(i * part, part)

    def remote(src, kind, slot, rows, number, i, offset):
        return pltpu.make_async_remote_copy(
            src_ref=src.at[rows], dst_ref=buf.at[kind, slot, rows],
            send_sem=send_sem.at[number, i], recv_sem=recv_sem.at[kind, slot, i],
            device_id=peer(offset), device_id_type=MESH)

    def landed(kind, slot, rows, i):
        pltpu.make_async_remote_copy(
            src_ref=buf.at[kind, slot, rows], dst_ref=buf.at[kind, slot, rows],
            send_sem=send_sem.at[0, i], recv_sem=recv_sem.at[kind, slot, i],
            device_id=peer(1), device_id_type=MESH).wait_recv()

    everything = pl.ds(0, count)
    scale = jnp.exp(jnp.full((1, 1), temp_ref[0], jnp.float32))
    shift = bias_ref[0]

    def tile(kind, visit, first):
        other = visit[...]
        dots = lax.dot_general(own[1 - kind], other, (((1,), (1,)), ((), ())),
                               preferred_element_type=jnp.float32)
        z = scale * dots + shift
        if first:
            eye = (lax.broadcasted_iota(jnp.int32, z.shape, 0)
                   == lax.broadcasted_iota(jnp.int32, z.shape, 1))
            z = jnp.where(eye, -z, z)
        e = jnp.exp(z)
        more = 1.0 + e
        soft = jnp.log(more)
        slope = (e / more) * scale
        if first:
            slope = jnp.where(eye, -slope, slope)
        wide = losses.shape[2]
        folded = soft[:, :wide]
        if first:
            for at in range(wide, count, wide):
                folded = folded + soft[:, at:at + wide]
        grad = jnp.dot(slope.astype(jnp.bfloat16), other, preferred_element_type=jnp.float32)
        if first:
            losses[kind] = folded
            acc[kind] = grad
        else:
            losses[kind] = losses[kind] + folded
            acc[kind] = acc[kind] + grad

    sent = []

    def send(copy, when=None):
        if when is None:
            copy.start()
        else:
            pl.when(when)(copy.start)
        sent.append((copy, when))

    for j in range(LOADS):
        normalise(q, j)
    pl.semaphore_wait(barrier, len(PEERS))
    for i in range(CHUNKS):
        send(remote(own.at[q], q, 2, rows_of(i), 6, i, -3), direct)
        send(remote(own.at[q], q, 0, rows_of(i), 0, i, -1))
    for j in range(LOADS):
        normalise(p, j)
    for i in range(CHUNKS):
        send(remote(own.at[p], p, 2, rows_of(i), 4, i, 3), early)
    send(remote(own.at[p], p, 0, everything, 1, 0, 1))

    tile(0, own.at[0], True)
    tile(1, own.at[1], True)
    span = count // HALVES

    def half_tile(kind, slot, h):
        tile(kind, buf.at[kind, slot, pl.ds(h * span, span)], False)

    landed(q, 0, everything, 0)
    for h in range(HALVES):
        half_tile(q, 0, h)

    late = jnp.logical_not(early)
    staying = jnp.logical_not(leaving)
    per = CHUNKS // HALVES

    def pass_on(i):
        landed(q, 2, rows_of(i), i)
        send(remote(buf.at[q, 2], q, 1, rows_of(i), 5, i, 1))

    for i in range(CHUNKS):
        rows = rows_of(i)
        landed(p, 0, rows, i)
        send(remote(buf.at[p, 0], p, 2, rows, 2, i, 2), staying)
        send(remote(buf.at[p, 0], p, 1, rows, 3, i, 1))
        again = remote(own.at[p], p, 2, rows, 4, i, 3)
        pl.when(late)(again.start)
        if i > 0:
            pass_on(i - 1)
        if i % per == per - 1:
            half_tile(p, 0, i // per)
        if i > 0 and (i - 1) % per == per - 1:
            half_tile(q, 2, (i - 1) // per)
    pass_on(CHUNKS - 1)
    half_tile(q, 2, HALVES - 1)
    for kind, slot in ((q, 1), (p, 1), (p, 2)):
        for h in range(HALVES):
            for i in range(h * per, (h + 1) * per):
                landed(kind, slot, rows_of(i), i)
            half_tile(kind, slot, h)

    loss_ref[...] = jnp.sum(losses[0].T, axis=0, keepdims=True) / (STEPS * count)
    for kind, out in ((0, gimg_ref), (1, gtxt_ref)):
        factor = inv[1 - kind][:, :1]
        unit = xin[1 - kind] * factor
        grad = acc[kind]
        along = jnp.sum(unit * grad, axis=-1, keepdims=True)
        out[...] = (grad - unit * along) * factor
    for copy, when in sent:
        if when is None or when is early:
            copy.wait_send()
        else:
            pl.when(when)(copy.wait_send)


def local(images, texts, log_temp, bias):
    count, width = images.shape
    block = jax.ShapeDtypeStruct((count, width), jnp.float32)
    vmem = pl.BlockSpec(memory_space=pltpu.VMEM)
    smem = pl.BlockSpec(memory_space=pltpu.SMEM)
    hbm = pl.BlockSpec(memory_space=pl.ANY)
    loss, gimg, gtxt = pl.pallas_call(
        kernel,
        out_shape=(jax.ShapeDtypeStruct((1, count), jnp.float32), block, block),
        in_specs=[hbm, hbm, smem, smem],
        out_specs=(vmem, vmem, vmem),
        scratch_shapes=[
            pltpu.VMEM((2, count, width), jnp.float32),
            pltpu.VMEM((2, count, width), jnp.bfloat16),
            pltpu.VMEM((2, STEPS - 1, count, width), jnp.bfloat16),
            pltpu.VMEM((2, count, width), jnp.float32),
            pltpu.VMEM((2, count, count // HALVES), jnp.float32),
            pltpu.VMEM((2, count, 128), jnp.float32),
            pltpu.SemaphoreType.DMA((2, LOADS)),
            pltpu.SemaphoreType.DMA((7, CHUNKS)),
            pltpu.SemaphoreType.DMA((2, STEPS - 1, CHUNKS)),
        ],
        compiler_params=pltpu.CompilerParams(
            collective_id=0, has_side_effects=True, vmem_limit_bytes=62 * 1024 * 1024),
    )(images, texts, log_temp, bias)
    return (loss.reshape(count), gimg, gtxt)


def solution(mesh):
    placed = (P(("dp", "rows"), None), P(("dp", "rows"), None), P(), P())
    return jax.shard_map(
        local,
        mesh=mesh,
        in_specs=placed,
        out_specs=(P(("dp", "rows")), P(("dp", "rows"), None), P(("dp", "rows"), None)),
        check_vma=False,
    )
```

time: 60 us -> 59.9 us (level)
    unnamed x7 -> x5, local copies, waits for them, and re-layouts: 5.12 us -> 4.71 us
where the time goes in v2:
time: 59.9 us; the launch traced here: 59.7 us
  Pallas kernels  53.1 us (89%)
  local copies, waits for them, and re-layouts  4.71 us (8%)
  between operations  1.93 us (3%)
    pallas_call x1, Pallas kernels, local(): pl.pallas_call(kernel, out_shape=(jax.ShapeDtypeStruct((1, count), jnp.fl...  53.1 us
    unnamed x5, local copies, waits for them, and re-layouts  4.71 us

profile of v2, /device:TPU:0, one launch (start us, length us, event | category | flops | bytes accessed | tf_op | source)
XLA Modules:
  0.0 59.7 jit_solution(4716533007993093387)
XLA Ops:
  1.9 53.1 %shard_map.67 = (f32[1,256]{1,0:T(1,128)}, f32[256,1152]{1,0:T(8,128)}, f32[256,1152]{1,0:T(8,128)}) custom-call(f32[256,1152]{1,0:T(8,128)} %img_hbm.1, f32[256,1152]{1,0:T(8,128)} %txt_hbm.1, f32[1]{0:T(128)S(6)} %copy.10.temp_ref, f32[1]{0:T(128)S(6)} %copy.11.bias_ref), custom_call_target="tpu_custom_call" | custom-call | tf_op jit(solution)/shard_map/pallas_call | solution.py:193
  55.0 1.2 %copy.12 = f32[256]{0:T(256)} copy(f32[256]{0:T(256)} %bitcast.1) | data formatting | bytes 2048
  56.2 0.0 copy-start
  56.2 2.5 %copy.13 = f32[256,1152]{1,0:T(8,128)} copy(f32[256,1152]{1,0:T(8,128)} %get-tuple-element.13) | data formatting | bytes 2359296
  58.7 0.0 copy-done
  58.7 1.0 %copy.14 = f32[256,1152]{1,0:T(8,128)} copy(f32[256,1152]{1,0:T(8,128)S(1)} %copy-done) | data formatting | bytes 2359296
Async XLA Ops:
  56.2 2.5 %copy-start = (f32[256,1152]{1,0:T(8,128)S(1)}, f32[256,1152]{1,0:T(8,128)}, u32[]{:S(2)}) copy-start(f32[256,1152]{1,0:T(8,128)} %get-tuple-element.14) | copy-start | bytes 3538948

commit v3 on v2

--- a/solution.py
+++ b/solution.py
@@ -11,6 +11,7 @@
 CHUNKS = 8
 HALVES = 2
 LOADS = 4
+LAG = 6
 PEERS = (1, 2, 3, -1, -2, -3)
 MESH = pl.DeviceIdType.MESH
 
@@ -59,7 +60,6 @@
         return jnp.logical_or(at + way < 0, at + way >= line)
 
     leaving = crosses(spot, d)
-    early = jnp.logical_or(leaving, crosses(spot, -d))
     direct = crosses(lax.rem(spot - d + line, line), -d)
 
     def rows_of(i):
@@ -122,12 +122,9 @@
         normalise(q, j)
     pl.semaphore_wait(barrier, len(PEERS))
     for i in range(CHUNKS):
-        send(remote(own.at[q], q, 2, rows_of(i), 6, i, -3), direct)
         send(remote(own.at[q], q, 0, rows_of(i), 0, i, -1))
     for j in range(LOADS):
         normalise(p, j)
-    for i in range(CHUNKS):
-        send(remote(own.at[p], p, 2, rows_of(i), 4, i, 3), early)
     send(remote(own.at[p], p, 0, everything, 1, 0, 1))
 
     tile(0, own.at[0], True)
@@ -141,30 +138,39 @@
     for h in range(HALVES):
         half_tile(q, 0, h)
 
-    late = jnp.logical_not(early)
     staying = jnp.logical_not(leaving)
     per = CHUNKS // HALVES
+
+    def second_wave(i):
+        rows = rows_of(i)
+        send(remote(buf.at[p, 0], p, 2, rows, 2, i, 2), staying)
+        send(remote(own.at[p], p, 2, rows, 4, i, 3))
+        send(remote(own.at[q], q, 2, rows, 6, i, -3), direct)
 
     def pass_on(i):
         landed(q, 2, rows_of(i), i)
         send(remote(buf.at[q, 2], q, 1, rows_of(i), 5, i, 1))
 
     for i in range(CHUNKS):
-        rows = rows_of(i)
-        landed(p, 0, rows, i)
-        send(remote(buf.at[p, 0], p, 2, rows, 2, i, 2), staying)
-        send(remote(buf.at[p, 0], p, 1, rows, 3, i, 1))
-        again = remote(own.at[p], p, 2, rows, 4, i, 3)
-        pl.when(late)(again.start)
-        if i > 0:
-            pass_on(i - 1)
+        landed(p, 0, rows_of(i), i)
+        send(remote(buf.at[p, 0], p, 1, rows_of(i), 3, i, 1))
+        if i >= LAG:
+            second_wave(i - LAG)
+    for i in range(CHUNKS - LAG, CHUNKS):
+        second_wave(i)
+    for h in range(HALVES):
+        half_tile(p, 0, h)
+    for h in range(HALVES):
+        for i in range(h * per, (h + 1) * per):
+            landed(q, 1, rows_of(i), i)
+        half_tile(q, 1, h)
+    for i in range(CHUNKS - 1):
+        pass_on(i)
         if i % per == per - 1:
-            half_tile(p, 0, i // per)
-        if i > 0 and (i - 1) % per == per - 1:
-            half_tile(q, 2, (i - 1) // per)
+            half_tile(q, 2, i // per)
     pass_on(CHUNKS - 1)
     half_tile(q, 2, HALVES - 1)
-    for kind, slot in ((q, 1), (p, 1), (p, 2)):
+    for kind, slot in ((p, 1), (p, 2)):
         for h in range(HALVES):
             for i in range(h * per, (h + 1) * per):
                 landed(kind, slot, rows_of(i), i)
@@ -178,10 +184,26 @@
         along = jnp.sum(unit * grad, axis=-1, keepdims=True)
         out[...] = (grad - unit * along) * factor
     for copy, when in sent:
-        if when is None or when is early:
+        if when is None:
             copy.wait_send()
         else:
             pl.when(when)(copy.wait_send)
+
+
+def hand_over(*refs):
+    half = (len(refs) - 1) // 2
+    sem = refs[-1]
+    copies = []
+    for number, (src, dst) in enumerate(zip(refs[:half], refs[half:-1])):
+        pieces = LOADS if src.shape[0] % LOADS == 0 else 1
+        length = src.shape[0] // pieces
+        for j in range(pieces):
+            rows = pl.ds(j * length, length)
+            copies.append(pltpu.make_async_copy(src.at[rows], dst.at[rows], sem.at[number, j]))
+    for copy in copies:
+        copy.start()
+    for copy in copies:
+        copy.wait()
 
 
 def local(images, texts, log_temp, bias):
@@ -209,6 +231,15 @@
         compiler_params=pltpu.CompilerParams(
             collective_id=0, has_side_effects=True, vmem_limit_bytes=62 * 1024 * 1024),
     )(images, texts, log_temp, bias)
+    results = (loss, gimg, gtxt)
+    loss, gimg, gtxt = pl.pallas_call(
+        hand_over,
+        out_shape=tuple(jax.ShapeDtypeStruct(value.shape, value.dtype) for value in results),
+        in_specs=[hbm] * 3,
+        out_specs=(hbm,) * 3,
+        scratch_shapes=[pltpu.SemaphoreType.DMA((3, LOADS))],
+        compiler_params=pltpu.CompilerParams(vmem_limit_bytes=62 * 1024 * 1024),
+    )(*results)
     return (loss.reshape(count), gimg, gtxt)
 
 

time: 59.9 us -> 126 us (2.10)
  Pallas kernels: 53.1 us -> 124 us
  local copies, waits for them, and re-layouts: 4.71 us -> 0 us
    pallas_call x0 -> x1, Pallas kernels: none -> 72.7 us  [local(): pl.pallas_call(hand_over, out_shape=tuple((jax.ShapeDtypeStruct(value.sha...]
    unnamed x5 -> x0, local copies, waits for them, and re-layouts: 4.71 us -> none
    pallas_call x1, Pallas kernels: 53.1 us -> 51.7 us  [local(): pl.pallas_call(kernel, out_shape=(jax.ShapeDtypeStruct((1, count), jnp.fl...]
where the time goes in v3:
time: 126 us
  Pallas kernels  124 us (98%)
  between operations  1.93 us (2%)
    pallas_call x1, Pallas kernels, local(): pl.pallas_call(hand_over, out_shape=tuple((jax.ShapeDtypeStruct(value.sha...  72.7 us
    pallas_call x1, Pallas kernels, local(): pl.pallas_call(kernel, out_shape=(jax.ShapeDtypeStruct((1, count), jnp.fl...  51.7 us

profile of v3, /device:TPU:0, one launch (start us, length us, event | category | flops | bytes accessed | tf_op | source)
XLA Modules:
  0.0 126.3 jit_solution(16758350438637164218)
XLA Ops:
  1.9 51.7 %shard_map.67 = (f32[1,256]{1,0:T(1,128)}, f32[256,1152]{1,0:T(8,128)}, f32[256,1152]{1,0:T(8,128)}) custom-call(f32[256,1152]{1,0:T(8,128)} %img_hbm.1, f32[256,1152]{1,0:T(8,128)} %txt_hbm.1, f32[1]{0:T(128)S(6)} %copy.7.temp_ref, f32[1]{0:T(128)S(6)} %copy.8.bias_ref), custom_call_target="tpu_custom_call" | custom-call | tf_op jit(solution)/shard_map/pallas_call | solution.py:215
  53.6 72.7 %shard_map.68 = (f32[1,256]{1,0:T(1,128)}, f32[256,1152]{1,0:T(8,128)}, f32[256,1152]{1,0:T(8,128)}) custom-call(f32[1,256]{1,0:T(1,128)} %get-tuple-element.9.refs_0_, f32[256,1152]{1,0:T(8,128)} %get-tuple-element.10.refs_1_, f32[256,1152]{1,0:T(8,128)} %get-tuple-element.11.refs_2_), custom_call_target="tpu_custom_call" | custom-call | tf_op jit(solution)/shard_map/pallas_call | solution.py:235

commit v4 on v3

--- a/solution.py
+++ b/solution.py
@@ -11,13 +11,14 @@
 CHUNKS = 8
 HALVES = 2
 LOADS = 4
+PIECES = 4
 LAG = 6
 PEERS = (1, 2, 3, -1, -2, -3)
 MESH = pl.DeviceIdType.MESH
 
 
-def kernel(img_hbm, txt_hbm, temp_ref, bias_ref, loss_ref, gimg_ref, gtxt_ref,
-           xin, own, buf, acc, losses, inv, in_sem, send_sem, recv_sem):
+def kernel(img_hbm, txt_hbm, temp_ref, bias_ref, loss_ref, grad_hbm,
+           out_sem, xin, own, buf, acc, losses, inv, in_sem, send_sem, recv_sem):
     rows_n = lax.axis_size("rows")
     total = lax.axis_size("dp") * rows_n
     me = lax.axis_index("dp") * rows_n + lax.axis_index("rows")
@@ -108,6 +109,20 @@
         else:
             losses[kind] = losses[kind] + folded
             acc[kind] = acc[kind] + grad
+
+    def result(kind, j):
+        rows = pl.ds(j * piece, piece)
+        return pltpu.make_async_copy(acc.at[kind, rows], grad_hbm.at[kind, rows], out_sem.at[kind, j])
+
+    def finish(kind):
+        for j in range(LOADS):
+            rows = pl.ds(j * piece, piece)
+            factor = inv[1 - kind, rows][:, :1]
+            unit = xin[1 - kind, rows] * factor
+            grad = acc[kind, rows]
+            along = jnp.sum(unit * grad, axis=-1, keepdims=True)
+            acc[kind, rows] = (grad - unit * along) * factor
+            result(kind, j).start()
 
     sent = []
 
@@ -170,6 +185,7 @@
             half_tile(q, 2, i // per)
     pass_on(CHUNKS - 1)
     half_tile(q, 2, HALVES - 1)
+    finish(q)
     for kind, slot in ((p, 1), (p, 2)):
         for h in range(HALVES):
             for i in range(h * per, (h + 1) * per):
@@ -177,33 +193,38 @@
             half_tile(kind, slot, h)
 
     loss_ref[...] = jnp.sum(losses[0].T, axis=0, keepdims=True) / (STEPS * count)
-    for kind, out in ((0, gimg_ref), (1, gtxt_ref)):
-        factor = inv[1 - kind][:, :1]
-        unit = xin[1 - kind] * factor
-        grad = acc[kind]
-        along = jnp.sum(unit * grad, axis=-1, keepdims=True)
-        out[...] = (grad - unit * along) * factor
+    finish(p)
     for copy, when in sent:
         if when is None:
             copy.wait_send()
         else:
             pl.when(when)(copy.wait_send)
-
-
-def hand_over(*refs):
-    half = (len(refs) - 1) // 2
-    sem = refs[-1]
-    copies = []
-    for number, (src, dst) in enumerate(zip(refs[:half], refs[half:-1])):
-        pieces = LOADS if src.shape[0] % LOADS == 0 else 1
-        length = src.shape[0] // pieces
-        for j in range(pieces):
-            rows = pl.ds(j * length, length)
-            copies.append(pltpu.make_async_copy(src.at[rows], dst.at[rows], sem.at[number, j]))
-    for copy in copies:
-        copy.start()
-    for copy in copies:
-        copy.wait()
+    for kind in (q, p):
+        for j in range(LOADS):
+            result(kind, j).wait()
+
+
+def hand_over(loss_ref, grad_hbm, row_ref, gimg_hbm, gtxt_hbm, held, in_sem, out_sem):
+    piece = held.shape[1] // PIECES
+    outs = (gimg_hbm, gtxt_hbm)
+    order = [(kind, j) for kind in range(2) for j in range(PIECES)]
+
+    def into(kind, j):
+        rows = pl.ds(j * piece, piece)
+        return pltpu.make_async_copy(grad_hbm.at[kind, rows], held.at[kind, rows], in_sem.at[kind, j])
+
+    def out_of(kind, j):
+        rows = pl.ds(j * piece, piece)
+        return pltpu.make_async_copy(held.at[kind, rows], outs[kind].at[rows], out_sem.at[kind, j])
+
+    for at in order:
+        into(*at).start()
+    row_ref[...] = loss_ref[...]
+    for at in order:
+        into(*at).wait()
+        out_of(*at).start()
+    for at in order:
+        out_of(*at).wait()
 
 
 def local(images, texts, log_temp, bias):
@@ -212,12 +233,14 @@
     vmem = pl.BlockSpec(memory_space=pltpu.VMEM)
     smem = pl.BlockSpec(memory_space=pltpu.SMEM)
     hbm = pl.BlockSpec(memory_space=pl.ANY)
-    loss, gimg, gtxt = pl.pallas_call(
+    loss, grads = pl.pallas_call(
         kernel,
-        out_shape=(jax.ShapeDtypeStruct((1, count), jnp.float32), block, block),
+        out_shape=(jax.ShapeDtypeStruct((1, count), jnp.float32),
+                   jax.ShapeDtypeStruct((2, count, width), jnp.float32)),
         in_specs=[hbm, hbm, smem, smem],
-        out_specs=(vmem, vmem, vmem),
+        out_specs=(vmem, hbm),
         scratch_shapes=[
+            pltpu.SemaphoreType.DMA((2, LOADS)),
             pltpu.VMEM((2, count, width), jnp.float32),
             pltpu.VMEM((2, count, width), jnp.bfloat16),
             pltpu.VMEM((2, STEPS - 1, count, width), jnp.bfloat16),
@@ -231,15 +254,18 @@
         compiler_params=pltpu.CompilerParams(
             collective_id=0, has_side_effects=True, vmem_limit_bytes=62 * 1024 * 1024),
     )(images, texts, log_temp, bias)
-    results = (loss, gimg, gtxt)
     loss, gimg, gtxt = pl.pallas_call(
         hand_over,
-        out_shape=tuple(jax.ShapeDtypeStruct(value.shape, value.dtype) for value in results),
-        in_specs=[hbm] * 3,
-        out_specs=(hbm,) * 3,
-        scratch_shapes=[pltpu.SemaphoreType.DMA((3, LOADS))],
+        out_shape=(jax.ShapeDtypeStruct((1, count), jnp.float32), block, block),
+        in_specs=[vmem, hbm],
+        out_specs=(vmem, hbm, hbm),
+        scratch_shapes=[
+            pltpu.VMEM((2, count, width), jnp.float32),
+            pltpu.SemaphoreType.DMA((2, PIECES)),
+            pltpu.SemaphoreType.DMA((2, PIECES)),
+        ],
         compiler_params=pltpu.CompilerParams(vmem_limit_bytes=62 * 1024 * 1024),
-    )(*results)
+    )(loss, grads)
     return (loss.reshape(count), gimg, gtxt)
 
 

time: 126 us -> 57.2 us (0.45)
  Pallas kernels: 124 us -> 55.1 us
    pallas_call x1, Pallas kernels: 72.7 us -> 3.73 us  [local(): pl.pallas_call(hand_over, out_shape=(jax.ShapeDtypeStruct((1, count), jnp...]
where the time goes in v4:
time: 57.2 us; the launch traced here: 57 us
  Pallas kernels  55.1 us (96%)
  between operations  1.93 us (3%)
    pallas_call x1, Pallas kernels, local(): pl.pallas_call(kernel, out_shape=(jax.ShapeDtypeStruct((1, count), jnp.fl...  51.4 us
    pallas_call x1, Pallas kernels, local(): pl.pallas_call(hand_over, out_shape=(jax.ShapeDtypeStruct((1, count), jnp...  3.73 us

profile of v4, /device:TPU:0, one launch (start us, length us, event | category | flops | bytes accessed | tf_op | source)
XLA Modules:
  0.0 57.0 jit_solution(2619175733547298832)
XLA Ops:
  1.9 51.4 %shard_map.67 = (f32[1,256]{1,0:T(1,128)}, f32[2,256,1152]{2,1,0:T(8,128)}) custom-call(f32[256,1152]{1,0:T(8,128)} %img_hbm.1, f32[256,1152]{1,0:T(8,128)} %txt_hbm.1, f32[1]{0:T(128)S(6)} %copy.7.temp_ref, f32[1]{0:T(128)S(6)} %copy.8.bias_ref), custom_call_target="tpu_custom_call" | custom-call | tf_op jit(solution)/shard_map/pallas_call | solution.py:236
  53.3 3.7 %shard_map.68 = (f32[1,256]{1,0:T(1,128)}, f32[256,1152]{1,0:T(8,128)}, f32[256,1152]{1,0:T(8,128)}) custom-call(f32[1,256]{1,0:T(1,128)} %get-tuple-element.8.loss_ref, f32[2,256,1152]{2,1,0:T(8,128)} %get-tuple-element.9.grad_hbm), custom_call_target="tpu_custom_call" | custom-call | tf_op jit(solution)/shard_map/pallas_call | solution.py:257

commit v5 on v3

--- a/solution.py
+++ b/solution.py
@@ -10,14 +10,14 @@
 STEPS = 4
 CHUNKS = 8
 HALVES = 2
-LOADS = 4
+PIECES = 4
 LAG = 6
 PEERS = (1, 2, 3, -1, -2, -3)
 MESH = pl.DeviceIdType.MESH
 
 
-def kernel(img_hbm, txt_hbm, temp_ref, bias_ref, loss_ref, gimg_ref, gtxt_ref,
-           xin, own, buf, acc, losses, inv, in_sem, send_sem, recv_sem):
+def kernel(img_ref, txt_ref, temp_ref, bias_ref, loss_ref, acc,
+           own, buf, losses, inv, send_sem, recv_sem):
     rows_n = lax.axis_size("rows")
     total = lax.axis_size("dp") * rows_n
     me = lax.axis_index("dp") * rows_n + lax.axis_index("rows")
@@ -35,23 +35,13 @@
     for offset in PEERS:
         pl.semaphore_signal(barrier, inc=1, device_id=peer(offset), device_id_type=MESH)
 
-    piece = count // LOADS
-
-    def loading(source, kind, j):
-        rows = pl.ds(j * piece, piece)
-        return pltpu.make_async_copy(source.at[rows], xin.at[kind, rows], in_sem.at[kind, j])
-
-    for j in range(LOADS):
-        loading(txt_hbm, 0, j).start()
-        loading(img_hbm, 1, j).start()
-
-    def normalise(kind, j):
-        rows = pl.ds(j * piece, piece)
-        loading(txt_hbm, kind, j).wait()
-        values = xin[kind, rows]
+    given = (txt_ref, img_ref)
+
+    def normalise(kind):
+        values = given[kind][...]
         scale_back = 1.0 / jnp.sqrt(jnp.sum(values * values, axis=-1, keepdims=True) + 1e-06)
-        inv[kind, rows] = jnp.broadcast_to(scale_back, (piece, inv.shape[2]))
-        own[kind, rows] = (values * scale_back).astype(jnp.bfloat16)
+        inv[kind] = jnp.broadcast_to(scale_back, inv.shape[1:])
+        own[kind] = (values * scale_back).astype(jnp.bfloat16)
 
     line = rows_n // 2
     spot = lax.rem(lax.div(me, 2), line)
@@ -109,6 +99,17 @@
             losses[kind] = losses[kind] + folded
             acc[kind] = acc[kind] + grad
 
+    def finish(kind):
+        factor = inv[1 - kind][:, :1]
+        unit = given[1 - kind][...] * factor
+        grad = acc[kind]
+        along = jnp.sum(unit * grad, axis=-1, keepdims=True)
+        acc[kind] = (grad - unit * along) * factor
+
+    def finish_one(dynamic):
+        for kind in range(2):
+            pl.when(dynamic == kind)(functools.partial(finish, kind))
+
     sent = []
 
     def send(copy, when=None):
@@ -118,13 +119,11 @@
             pl.when(when)(copy.start)
         sent.append((copy, when))
 
-    for j in range(LOADS):
-        normalise(q, j)
+    normalise(0)
+    normalise(1)
     pl.semaphore_wait(barrier, len(PEERS))
     for i in range(CHUNKS):
         send(remote(own.at[q], q, 0, rows_of(i), 0, i, -1))
-    for j in range(LOADS):
-        normalise(p, j)
     send(remote(own.at[p], p, 0, everything, 1, 0, 1))
 
     tile(0, own.at[0], True)
@@ -170,6 +169,7 @@
             half_tile(q, 2, i // per)
     pass_on(CHUNKS - 1)
     half_tile(q, 2, HALVES - 1)
+    finish_one(q)
     for kind, slot in ((p, 1), (p, 2)):
         for h in range(HALVES):
             for i in range(h * per, (h + 1) * per):
@@ -177,12 +177,7 @@
             half_tile(kind, slot, h)
 
     loss_ref[...] = jnp.sum(losses[0].T, axis=0, keepdims=True) / (STEPS * count)
-    for kind, out in ((0, gimg_ref), (1, gtxt_ref)):
-        factor = inv[1 - kind][:, :1]
-        unit = xin[1 - kind] * factor
-        grad = acc[kind]
-        along = jnp.sum(unit * grad, axis=-1, keepdims=True)
-        out[...] = (grad - unit * along) * factor
+    finish_one(p)
     for copy, when in sent:
         if when is None:
             copy.wait_send()
@@ -190,18 +185,16 @@
             pl.when(when)(copy.wait_send)
 
 
-def hand_over(*refs):
-    half = (len(refs) - 1) // 2
-    sem = refs[-1]
+def hand_over(loss_ref, grad_ref, row_ref, gimg_hbm, gtxt_hbm, sem):
+    piece = grad_ref.shape[1] // PIECES
     copies = []
-    for number, (src, dst) in enumerate(zip(refs[:half], refs[half:-1])):
-        pieces = LOADS if src.shape[0] % LOADS == 0 else 1
-        length = src.shape[0] // pieces
-        for j in range(pieces):
-            rows = pl.ds(j * length, length)
-            copies.append(pltpu.make_async_copy(src.at[rows], dst.at[rows], sem.at[number, j]))
+    for kind, out in enumerate((gimg_hbm, gtxt_hbm)):
+        for j in range(PIECES):
+            rows = pl.ds(j * piece, piece)
+            copies.append(pltpu.make_async_copy(grad_ref.at[kind, rows], out.at[rows], sem.at[kind, j]))
     for copy in copies:
         copy.start()
+    row_ref[...] = loss_ref[...]
     for copy in copies:
         copy.wait()
 
@@ -212,34 +205,33 @@
     vmem = pl.BlockSpec(memory_space=pltpu.VMEM)
     smem = pl.BlockSpec(memory_space=pltpu.SMEM)
     hbm = pl.BlockSpec(memory_space=pl.ANY)
-    loss, gimg, gtxt = pl.pallas_call(
+    loss, grads = pl.pallas_call(
         kernel,
-        out_shape=(jax.ShapeDtypeStruct((1, count), jnp.float32), block, block),
-        in_specs=[hbm, hbm, smem, smem],
-        out_specs=(vmem, vmem, vmem),
+        out_shape=(jax.ShapeDtypeStruct((1, count), jnp.float32),
+                   jax.ShapeDtypeStruct((2, count, width), jnp.float32)),
+        in_specs=[vmem, vmem, smem, smem],
+        out_specs=(vmem, vmem),
         scratch_shapes=[
-            pltpu.VMEM((2, count, width), jnp.float32),
             pltpu.VMEM((2, count, width), jnp.bfloat16),
             pltpu.VMEM((2, STEPS - 1, count, width), jnp.bfloat16),
-            pltpu.VMEM((2, count, width), jnp.float32),
             pltpu.VMEM((2, count, count // HALVES), jnp.float32),
             pltpu.VMEM((2, count, 128), jnp.float32),
-            pltpu.SemaphoreType.DMA((2, LOADS)),
             pltpu.SemaphoreType.DMA((7, CHUNKS)),
             pltpu.SemaphoreType.DMA((2, STEPS - 1, CHUNKS)),
         ],
         compiler_params=pltpu.CompilerParams(
-            collective_id=0, has_side_effects=True, vmem_limit_bytes=62 * 1024 * 1024),
+            collective_id=0, has_side_effects=True, vmem_limit_bytes=48 * 1024 * 1024),
     )(images, texts, log_temp, bias)
-    results = (loss, gimg, gtxt)
     loss, gimg, gtxt = pl.pallas_call(
         hand_over,
-        out_shape=tuple(jax.ShapeDtypeStruct(value.shape, value.dtype) for value in results),
-        in_specs=[hbm] * 3,
-        out_specs=(hbm,) * 3,
-        scratch_shapes=[pltpu.SemaphoreType.DMA((3, LOADS))],
-        compiler_params=pltpu.CompilerParams(vmem_limit_bytes=62 * 1024 * 1024),
-    )(*results)
+        out_shape=(jax.ShapeDtypeStruct((1, count), jnp.float32), block, block),
+        in_specs=[vmem, vmem],
+        out_specs=(vmem, hbm, hbm),
+        scratch_shapes=[
+            pltpu.SemaphoreType.DMA((2, PIECES)),
+        ],
+        compiler_params=pltpu.CompilerParams(vmem_limit_bytes=16 * 1024 * 1024),
+    )(loss, grads)
     return (loss.reshape(count), gimg, gtxt)
 
 

time: 126 us -> 57.7 us (0.46)
  Pallas kernels: 124 us -> 53 us
  local copies, waits for them, and re-layouts: 0 us -> 2.53 us
    pallas_call x1, Pallas kernels: 72.7 us -> 2.03 us  [local(): pl.pallas_call(hand_over, out_shape=(jax.ShapeDtypeStruct((1, count), jnp...]
    unnamed x0 -> x4, local copies, waits for them, and re-layouts: none -> 2.53 us
where the time goes in v5:
time: 57.7 us; the launch traced here: 57.5 us
  Pallas kernels  53 us (92%)
  local copies, waits for them, and re-layouts  2.53 us (4%)
  between operations  1.94 us (3%)
    pallas_call x1, Pallas kernels, local(): pl.pallas_call(kernel, out_shape=(jax.ShapeDtypeStruct((1, count), jnp.fl...  51 us
    unnamed x4, local copies, waits for them, and re-layouts  2.53 us
    pallas_call x1, Pallas kernels, local(): pl.pallas_call(hand_over, out_shape=(jax.ShapeDtypeStruct((1, count), jnp...  2.03 us

profile of v5, /device:TPU:0, one launch (start us, length us, event | category | flops | bytes accessed | tf_op | source)
XLA Modules:
  0.0 57.5 jit_solution(4968071575415133942)
XLA Ops:
  1.9 0.0 copy-start
  1.9 1.3 %copy-done = f32[256,1152]{1,0:T(8,128)S(1)} copy-done((f32[256,1152]{1,0:T(8,128)S(1)}, f32[256,1152]{1,0:T(8,128)}, u32[]{:S(2)}) %copy-start) | copy-done | bytes 1179672
  3.2 0.0 copy-start.1
  3.2 1.3 %copy-done.1 = f32[256,1152]{1,0:T(8,128)S(1)} copy-done((f32[256,1152]{1,0:T(8,128)S(1)}, f32[256,1152]{1,0:T(8,128)}, u32[]{:S(2)}) %copy-start.1) | copy-done | bytes 1179672
  4.5 51.0 %shard_map.67 = (f32[1,256]{1,0:T(1,128)S(1)}, f32[2,256,1152]{2,1,0:T(8,128)S(1)}) custom-call(f32[256,1152]{1,0:T(8,128)S(1)} %copy-done, f32[256,1152]{1,0:T(8,128)S(1)} %copy-done.1, f32[1]{0:T(128)S(6)} %copy.7.temp_ref, f32[1]{0:T(128)S(6)} %copy.8.bias_ref), custom_call_target="tpu_custom_call" | custom-call | tf_op jit(solution)/shard_map/pallas_call | solution.py:208
  55.4 2.0 %shard_map.68 = (f32[1,256]{1,0:T(1,128)}, f32[256,1152]{1,0:T(8,128)}, f32[256,1152]{1,0:T(8,128)}) custom-call(f32[1,256]{1,0:T(1,128)S(1)} %get-tuple-element.8.loss_ref, f32[2,256,1152]{2,1,0:T(8,128)S(1)} %get-tuple-element.9.grad_ref), custom_call_target="tpu_custom_call" | custom-call | tf_op jit(solution)/shard_map/pallas_call | solution.py:225
Async XLA Ops:
  1.9 1.3 %copy-start = (f32[256,1152]{1,0:T(8,128)S(1)}, f32[256,1152]{1,0:T(8,128)}, u32[]{:S(2)}) copy-start(f32[256,1152]{1,0:T(8,128)} %img_ref.1) | copy-start | bytes 3538948
  3.2 1.3 %copy-start.1 = (f32[256,1152]{1,0:T(8,128)S(1)}, f32[256,1152]{1,0:T(8,128)}, u32[]{:S(2)}) copy-start(f32[256,1152]{1,0:T(8,128)} %txt_ref.1) | copy-start | bytes 3538948

commit v6 on v5

--- a/solution.py
+++ b/solution.py
@@ -11,7 +11,8 @@
 CHUNKS = 8
 HALVES = 2
 PIECES = 4
-LAG = 6
+FAR_LAG = 3
+NEAR_LAG = 6
 PEERS = (1, 2, 3, -1, -2, -3)
 MESH = pl.DeviceIdType.MESH
 
@@ -140,11 +141,17 @@
     staying = jnp.logical_not(leaving)
     per = CHUNKS // HALVES
 
-    def second_wave(i):
+    def far_wave(i):
+        rows = rows_of(i)
+        send(remote(own.at[q], q, 2, rows, 6, i, -3), direct)
+        pl.when(leaving)(remote(own.at[p], p, 2, rows, 4, i, 3).start)
+
+    def near_wave(i):
         rows = rows_of(i)
         send(remote(buf.at[p, 0], p, 2, rows, 2, i, 2), staying)
-        send(remote(own.at[p], p, 2, rows, 4, i, 3))
-        send(remote(own.at[q], q, 2, rows, 6, i, -3), direct)
+        own_copy = remote(own.at[p], p, 2, rows, 4, i, 3)
+        pl.when(staying)(own_copy.start)
+        sent.append((own_copy, None))
 
     def pass_on(i):
         landed(q, 2, rows_of(i), i)
@@ -153,10 +160,14 @@
     for i in range(CHUNKS):
         landed(p, 0, rows_of(i), i)
         send(remote(buf.at[p, 0], p, 1, rows_of(i), 3, i, 1))
-        if i >= LAG:
-            second_wave(i - LAG)
-    for i in range(CHUNKS - LAG, CHUNKS):
-        second_wave(i)
+        if i >= FAR_LAG:
+            far_wave(i - FAR_LAG)
+        if i >= NEAR_LAG:
+            near_wave(i - NEAR_LAG)
+    for i in range(CHUNKS - FAR_LAG, CHUNKS):
+        far_wave(i)
+    for i in range(CHUNKS - NEAR_LAG, CHUNKS):
+        near_wave(i)
     for h in range(HALVES):
         half_tile(p, 0, h)
     for h in range(HALVES):

time: 57.7 us -> 57.7 us (level)
  no operation moved by 1% of the time
where the time goes in v6:
time: 57.7 us; the launch traced here: 57.5 us
  Pallas kernels  53 us (92%)
  local copies, waits for them, and re-layouts  2.53 us (4%)
  between operations  1.94 us (3%)
    pallas_call x1, Pallas kernels, local(): pl.pallas_call(kernel, out_shape=(jax.ShapeDtypeStruct((1, count), jnp.fl...  51 us
    unnamed x4, local copies, waits for them, and re-layouts  2.53 us
    pallas_call x1, Pallas kernels, local(): pl.pallas_call(hand_over, out_shape=(jax.ShapeDtypeStruct((1, count), jnp...  2.03 us

profile of v6, /device:TPU:0, one launch (start us, length us, event | category | flops | bytes accessed | tf_op | source)
XLA Modules:
  0.0 57.5 jit_solution(18133039386077736921)
XLA Ops:
  1.9 0.0 copy-start
  1.9 1.3 %copy-done = f32[256,1152]{1,0:T(8,128)S(1)} copy-done((f32[256,1152]{1,0:T(8,128)S(1)}, f32[256,1152]{1,0:T(8,128)}, u32[]{:S(2)}) %copy-start) | copy-done | bytes 1179672
  3.2 0.0 copy-start.1
  3.2 1.3 %copy-done.1 = f32[256,1152]{1,0:T(8,128)S(1)} copy-done((f32[256,1152]{1,0:T(8,128)S(1)}, f32[256,1152]{1,0:T(8,128)}, u32[]{:S(2)}) %copy-start.1) | copy-done | bytes 1179672
  4.5 51.0 %shard_map.67 = (f32[1,256]{1,0:T(1,128)S(1)}, f32[2,256,1152]{2,1,0:T(8,128)S(1)}) custom-call(f32[256,1152]{1,0:T(8,128)S(1)} %copy-done, f32[256,1152]{1,0:T(8,128)S(1)} %copy-done.1, f32[1]{0:T(128)S(6)} %copy.7.temp_ref, f32[1]{0:T(128)S(6)} %copy.8.bias_ref), custom_call_target="tpu_custom_call" | custom-call | tf_op jit(solution)/shard_map/pallas_call | solution.py:219
  55.4 2.0 %shard_map.68 = (f32[1,256]{1,0:T(1,128)}, f32[256,1152]{1,0:T(8,128)}, f32[256,1152]{1,0:T(8,128)}) custom-call(f32[1,256]{1,0:T(1,128)S(1)} %get-tuple-element.8.loss_ref, f32[2,256,1152]{2,1,0:T(8,128)S(1)} %get-tuple-element.9.grad_ref), custom_call_target="tpu_custom_call" | custom-call | tf_op jit(solution)/shard_map/pallas_call | solution.py:236
Async XLA Ops:
  1.9 1.3 %copy-start = (f32[256,1152]{1,0:T(8,128)S(1)}, f32[256,1152]{1,0:T(8,128)}, u32[]{:S(2)}) copy-start(f32[256,1152]{1,0:T(8,128)} %img_ref.1) | copy-start | bytes 3538948
  3.2 1.3 %copy-start.1 = (f32[256,1152]{1,0:T(8,128)S(1)}, f32[256,1152]{1,0:T(8,128)}, u32[]{:S(2)}) copy-start(f32[256,1152]{1,0:T(8,128)} %txt_ref.1) | copy-start | bytes 3538948

commit v7 on v6

--- a/solution.py
+++ b/solution.py
@@ -120,11 +120,15 @@
             pl.when(when)(copy.start)
         sent.append((copy, when))
 
-    normalise(0)
-    normalise(1)
+    def normalise_one(dynamic):
+        for kind in range(2):
+            pl.when(dynamic == kind)(functools.partial(normalise, kind))
+
+    normalise_one(q)
     pl.semaphore_wait(barrier, len(PEERS))
     for i in range(CHUNKS):
         send(remote(own.at[q], q, 0, rows_of(i), 0, i, -1))
+    normalise_one(p)
     send(remote(own.at[p], p, 0, everything, 1, 0, 1))
 
     tile(0, own.at[0], True)

time: 57.7 us -> 57.7 us (level)
  no operation moved by 1% of the time
where the time goes in v7:
time: 57.7 us; the launch traced here: 57.5 us
  Pallas kernels  53 us (92%)
  local copies, waits for them, and re-layouts  2.53 us (4%)
  between operations  1.94 us (3%)
    pallas_call x1, Pallas kernels, local(): pl.pallas_call(kernel, out_shape=(jax.ShapeDtypeStruct((1, count), jnp.fl...  51 us
    unnamed x4, local copies, waits for them, and re-layouts  2.53 us
    pallas_call x1, Pallas kernels, local(): pl.pallas_call(hand_over, out_shape=(jax.ShapeDtypeStruct((1, count), jnp...  2.03 us

profile of v7, /device:TPU:0, one launch (start us, length us, event | category | flops | bytes accessed | tf_op | source)
XLA Modules:
  0.0 57.5 jit_solution(5220081317510033554)
XLA Ops:
  1.9 0.0 copy-start
  1.9 1.3 %copy-done = f32[256,1152]{1,0:T(8,128)S(1)} copy-done((f32[256,1152]{1,0:T(8,128)S(1)}, f32[256,1152]{1,0:T(8,128)}, u32[]{:S(2)}) %copy-start) | copy-done | bytes 1179672
  3.2 0.0 copy-start.1
  3.2 1.3 %copy-done.1 = f32[256,1152]{1,0:T(8,128)S(1)} copy-done((f32[256,1152]{1,0:T(8,128)S(1)}, f32[256,1152]{1,0:T(8,128)}, u32[]{:S(2)}) %copy-start.1) | copy-done | bytes 1179672
  4.5 51.0 %shard_map.67 = (f32[1,256]{1,0:T(1,128)S(1)}, f32[2,256,1152]{2,1,0:T(8,128)S(1)}) custom-call(f32[256,1152]{1,0:T(8,128)S(1)} %copy-done, f32[256,1152]{1,0:T(8,128)S(1)} %copy-done.1, f32[1]{0:T(128)S(6)} %copy.7.temp_ref, f32[1]{0:T(128)S(6)} %copy.8.bias_ref), custom_call_target="tpu_custom_call" | custom-call | tf_op jit(solution)/shard_map/pallas_call | solution.py:223
  55.4 2.0 %shard_map.68 = (f32[1,256]{1,0:T(1,128)}, f32[256,1152]{1,0:T(8,128)}, f32[256,1152]{1,0:T(8,128)}) custom-call(f32[1,256]{1,0:T(1,128)S(1)} %get-tuple-element.8.loss_ref, f32[2,256,1152]{2,1,0:T(8,128)S(1)} %get-tuple-element.9.grad_ref), custom_call_target="tpu_custom_call" | custom-call | tf_op jit(solution)/shard_map/pallas_call | solution.py:240
Async XLA Ops:
  1.9 1.3 %copy-start = (f32[256,1152]{1,0:T(8,128)S(1)}, f32[256,1152]{1,0:T(8,128)}, u32[]{:S(2)}) copy-start(f32[256,1152]{1,0:T(8,128)} %img_ref.1) | copy-start | bytes 3538948
  3.2 1.3 %copy-start.1 = (f32[256,1152]{1,0:T(8,128)S(1)}, f32[256,1152]{1,0:T(8,128)}, u32[]{:S(2)}) copy-start(f32[256,1152]{1,0:T(8,128)} %txt_ref.1) | copy-start | bytes 3538948
